TPU v7x, 32 devices: a whole 2x2x4 slice. The times are simulated.
32 devices in a mesh: row: 4 (over z), col: 8 (over y, x, core).
Axes of the slice: x: 2, y: 2, z: 4, core: 2. Of those that a mesh axis runs over, the one named last changes fastest.
Arguments:
- source_tiles: bfloat16 [4, 8, 1024, 128], P('row', 'col'), may hold values from -6 to 6
- requests: int32 [4, 8, 8, 256], P('row', 'col'), may hold values from 0 to 1023
- stencil: int32 [128, 256, 4], P('row', 'col'), may hold values from 0 to 2047, as said below
- regrid_weight: float32 [128, 256, 4], P('row', 'col'), may hold values from 0.1 to 0.6
- w_in: bfloat16 [3, 3, 64, 128], replicated, may hold values from -0.4375 to 0.4375
- w_enc: bfloat16 [3, 3, 128, 128], replicated, may hold values from -0.3125 to 0.3125
- w_mid_first: bfloat16 [3, 3, 128, 128], replicated, may hold values from -0.3125 to 0.3125
- w_mid_second: bfloat16 [3, 3, 128, 128], replicated, may hold values from -0.3125 to 0.3125
- w_dec_first: bfloat16 [3, 3, 256, 128], replicated, may hold values from -0.21875 to 0.21875
- w_dec_second: bfloat16 [3, 3, 128, 128], replicated, may hold values from -0.3125 to 0.3125
- w_out: bfloat16 [128, 64], replicated, may hold values from -0.75 to 0.75
Outputs:
- forecast: bfloat16 [128, 256, 2, 64], P('row', 'col')
Inputs may be any that keep to these rules, and one draw needn't show every extreme that they name: `stencil`: within each device's 32 x 32 block of target cells, every slot 0 to 2047 appears at least once among the entries.
All inputs are finite; a program needn't handle non-finite values.
Results may differ from a plain program's by a relative error of at most 0.017.
Values may be sent and summed in bfloat16 or wider, within the bound.
A program may use at most 64 MiB of HBM per device.

v0:
```python
import jax
import jax.numpy as jnp
from jax import lax
from jax.sharding import PartitionSpec as P

FIELDS = 64
CH = 128


def with_halo(x, sides, width):
    for axis, dim in sides:
        devices, length = (lax.axis_size(axis), x.shape[dim])
        up = [(i, (i + 1) % devices) for i in range(devices)]
        down = [(j, i) for i, j in up]
        last = lax.slice_in_dim(x, length - width, length, axis=dim)
        leading = lax.slice_in_dim(x, 0, width, axis=dim)
        before = lax.ppermute(last, axis, up)
        after = lax.ppermute(leading, axis, down)
        x = jnp.concatenate([before, x, after], axis=dim)
    return x


def conv_valid(padded, weight):
    height = padded.shape[0] - 2
    width = padded.shape[1] - 2
    samples = padded.shape[2]
    inner = padded.shape[3]
    outer = weight.shape[3]
    total = jnp.zeros((height * width * samples, outer), jnp.float32)
    for row_step in range(3):
        for col_step in range(3):
            window = padded[row_step : row_step + height, col_step : col_step + width].reshape(
                -1, inner
            )
            total = total + jnp.dot(
                window, weight[row_step, col_step], preferred_element_type=jnp.float32
            )
    return jax.nn.silu(total).reshape(height, width, samples, outer).astype(jnp.bfloat16)


def rim_clear(padded, depth, rows_dev):
    global_rows = (
        lax.axis_index("row") * rows_dev + jnp.arange(padded.shape[0], dtype=jnp.int32) - depth
    )
    inside = (global_rows >= 0) & (global_rows < lax.axis_size("row") * rows_dev)
    return jnp.where(inside[:, None, None, None], padded, jnp.zeros_like(padded))


def body(
    source_tiles,
    requests,
    stencil,
    regrid_weight,
    w_in,
    w_enc,
    w_mid_first,
    w_mid_second,
    w_dec_first,
    w_dec_second,
    w_out,
):
    tile_rows = stencil.shape[0]
    tile_cols = stencil.shape[1]
    columns = source_tiles.shape[3]
    samples = columns // FIELDS
    cells = source_tiles.shape[2]
    groups = requests.shape[2]
    capacity = requests.shape[3]
    wanted = requests.reshape(groups, capacity)
    global_ids = (jnp.arange(groups, dtype=jnp.int32)[:, None] * cells + wanted).reshape(-1)
    empty = jnp.zeros((groups * capacity, columns), jnp.bfloat16)
    flattened = lax.all_gather(source_tiles, "col", axis=1, tiled=True).reshape(-1, columns)
    inside = (global_ids >= 0) & (global_ids < flattened.shape[0])
    picked = flattened[jnp.clip(global_ids, 0, flattened.shape[0] - 1)]
    buffer = jnp.where(inside[:, None], picked, empty)
    picked = buffer[stencil]
    regridded = jnp.sum(picked.astype(jnp.float32) * regrid_weight[..., None], axis=2).astype(
        jnp.bfloat16
    )
    regridded = regridded.reshape(tile_rows, tile_cols, samples, FIELDS)
    padded = rim_clear(with_halo(regridded, (("row", 0), ("col", 1)), 1), 1, tile_rows)
    first = conv_valid(padded, w_in)
    padded = rim_clear(with_halo(first, (("row", 0), ("col", 1)), 1), 1, tile_rows)
    skip = conv_valid(padded, w_enc)
    half_rows = tile_rows // 2
    half_cols = tile_cols // 2
    pooled = (
        skip.astype(jnp.float32)
        .reshape(half_rows, 2, half_cols, 2, samples, CH)
        .mean(axis=(1, 3))
        .astype(jnp.bfloat16)
    )
    padded = rim_clear(with_halo(pooled, (("row", 0), ("col", 1)), 1), 1, half_rows)
    middle = conv_valid(padded, w_mid_first)
    padded = rim_clear(with_halo(middle, (("row", 0), ("col", 1)), 1), 1, half_rows)
    coarse = conv_valid(padded, w_mid_second)
    upsampled = jnp.repeat(jnp.repeat(coarse, 2, axis=0), 2, axis=1)
    joined = jnp.concatenate([upsampled, skip], axis=-1)
    padded = rim_clear(with_halo(joined, (("row", 0), ("col", 1)), 1), 1, tile_rows)
    decoded_first = conv_valid(padded, w_dec_first)
    padded = rim_clear(with_halo(decoded_first, (("row", 0), ("col", 1)), 1), 1, tile_rows)
    decoded = conv_valid(padded, w_dec_second)
    result = jnp.dot(decoded.reshape(-1, CH), w_out, preferred_element_type=jnp.float32)
    return result.reshape(tile_rows, tile_cols, samples, FIELDS).astype(jnp.bfloat16)


def solution(mesh):
    placed = (
        P("row", "col", None, None),
        P("row", "col", None, None),
        P("row", "col", None),
        P("row", "col", None),
        P(),
        P(),
        P(),
        P(),
        P(),
        P(),
        P(),
    )
    return jax.shard_map(
        body, mesh=mesh, in_specs=placed, out_specs=P("row", "col", None, None), check_vma=False
    )
```

profile of v0, /device:TPU:3, one launch (start us, length us, event | category | flops | bytes accessed | tf_op | source)
XLA Modules:
  0.0 215.8 jit_solution(13235562589627824381)
XLA Ops:
  11.3 27.5 %all-gather.2.cloned.1.call-done = bf16[1,8,1024,128]{3,2,0,1:T(8,128)(2,1)} async-done(((bf16[1,1,1024,128]{3,2,0,1:T(8,128)(2,1)}), bf16[1,8,1024,128]{3,2,0,1:T(8,128)(2,1)}) %all-gather.2.cloned.1.call-update) | async-done | bytes 2097168 | tf_op jit(solution)/shard_map/all_gather | solution.py:72
  38.8 7.5 %gather_fusion = bf16[2048,128]{1,0:T(8,128)(2,1)S(1)} fusion(bf16[8192,128]{1,0:T(8,128)(2,1)} %bitcast.301, s32[2048]{0:T(1024)S(1)} %broadcast_clamp_fusion.1), kind=kCustom, calls=%fused_computation | custom fusion | bytes 1056768 | tf_op jit(solution)/shard_map/gather | solution.py:74
  46.6 12.1 %gather_fusion.1 = bf16[4096,128]{1,0:T(8,128)(2,1)S(1)} fusion(bf16[2048,128]{1,0:T(8,128)(2,1)S(1)} %broadcast_select_fusion.4, s32[4096]{0:T(1024)S(1)} %broadcast_clamp_fusion), kind=kCustom, calls=%fused_computation.1 | custom fusion | bytes 2113536 | tf_op jit(solution)/shard_map/gather | solution.py:76
  65.5 2.6 %collective-permute-start.2 = (bf16[34,1,2,64]{3,2,1,0:T(2,128)(2,1)S(1)}, bf16[34,1,2,64]{3,2,1,0:T(2,128)(2,1)S(1)}, u32[]{:S(2)}, u32[]{:S(2)}) collective-permute-start(bf16[34,1,2,64]{3,2,1,0:T(2,128)(2,1)S(1)} %get-tuple-element.49), channel_id=1, source_target_pairs={{0,1},{1,2},{2,3},{3,4},{4,5},{5,6},{6,7},{7,0},{8,9},{9,10},{10,1... | collective-permute-start | bytes 26120 | tf_op jit(solution)/shard_map/ppermute | solution.py:17
  69.0 3.2 %collective-permute-done.3 = bf16[34,1,2,64]{3,2,1,0:T(2,128)(2,1)S(1)} collective-permute-done((bf16[34,1,2,64]{3,2,1,0:T(2,128)(2,1)S(1)}, bf16[34,1,2,64]{3,2,1,0:T(2,128)(2,1)S(1)}, u32[]{:S(2)}, u32[]{:S(2)}) %collective-permute-start.3) | collective-permute-done | bytes 8736 | tf_op jit(solution)/shard_map/ppermute | solution.py:18
  73.3 5.2 %fusion.120 = (bf16[32,32,2,64]{3,2,1,0:T(2,128)(2,1)S(1)}, bf16[32,32,2,64]{3,2,1,0:T(2,128)(2,1)S(1)}, bf16[32,32,2,64]{3,2,1,0:T(2,128)(2,1)S(1)}, bf16[32,32...) fusion(bf16[34,34,2,64]{3,2,1,0:T(2,128)(2,1)S(1)} %broadcast_s, ...), kind=kLoop, calls=%fused_computation.218 | loop fusion | bytes 4718592 | tf_op jit(solution)/shard_map/slice | solution.py:32
  81.2 3.2 %collective-permute-start.5 = (bf16[1,32,2,128]{3,2,1,0:T(2,128)(2,1)S(1)}, bf16[1,32,2,128]{3,2,1,0:T(2,128)(2,1)S(1)}, u32[]{:S(2)}, u32[]{:S(2)}) collective-permute-start(bf16[1,32,2,128]{3,2,1,0:T(2,128)(2,1)S(1)} %bitcast.373), channel_id=1, source_target_pairs={{8,0},{16,8},{24,16},{0,24},{9,1},{17,9},{25,17},{1,25},{10,2},{18... | collective-permute-start | bytes 49160 | tf_op jit(solution)/shard_map/ppermute | solution.py:18
  85.3 3.5 %collective-permute-done.4 = bf16[1,32,2,128]{3,2,1,0:T(2,128)(2,1)S(1)} collective-permute-done((bf16[1,32,2,128]{3,2,1,0:T(2,128)(2,1)S(1)}, bf16[1,32,2,128]{3,2,1,0:T(2,128)(2,1)S(1)}, u32[]{:S(2)}, u32[]{:S(2)}) %collective-permute-start.4) | collective-permute-done | bytes 16416 | tf_op jit(solution)/shard_map/ppermute | solution.py:17
  91.2 3.2 %collective-permute-done.7 = bf16[34,1,2,128]{3,2,1,0:T(2,128)(2,1)S(1)} collective-permute-done((bf16[34,1,2,128]{3,2,1,0:T(2,128)(2,1)S(1)}, bf16[34,1,2,128]{3,2,1,0:T(2,128)(2,1)S(1)}, u32[]{:S(2)}, u32[]{:S(2)}) %collective-permute-start.7) | collective-permute-done | bytes 17440 | tf_op jit(solution)/shard_map/ppermute | solution.py:18
  96.2 5.2 %fusion.119 = (bf16[32,32,2,128]{3,2,1,0:T(2,128)(2,1)S(1)}, bf16[32,32,2,128]{3,2,1,0:T(2,128)(2,1)S(1)}, bf16[32,32,2,128]{3,2,1,0:T(2,128)(2,1)S(1)}, bf16[32...) fusion(bf16[34,34,2,128]{3,2,1,0:T(2,128)(2,1)S(1)} %broadcast_, ...), kind=kLoop, calls=%fused_computation.217 | loop fusion | bytes 9437184 | tf_op jit(solution)/shard_map/slice | solution.py:32
  104.9 3.3 %collective-permute-start.9 = (bf16[1,16,2,128]{3,2,1,0:T(2,128)(2,1)S(1)}, bf16[1,16,2,128]{3,2,1,0:T(2,128)(2,1)S(1)}, u32[]{:S(2)}, u32[]{:S(2)}) collective-permute-start(bf16[1,16,2,128]{3,2,1,0:T(2,128)(2,1)S(1)} %get-tuple-element.82), channel_id=1, source_target_pairs={{8,0},{16,8},{24,16},{0,24},{9,1},{17,9},{25,17},{1,25},{10,2},{18... | collective-permute-start | bytes 24584 | tf_op jit(solution)/shard_map/ppermute | solution.py:18
  111.4 3.2 %collective-permute-done.11 = bf16[18,1,2,128]{3,2,1,0:T(2,128)(2,1)S(1)} collective-permute-done((bf16[18,1,2,128]{3,2,1,0:T(2,128)(2,1)S(1)}, bf16[18,1,2,128]{3,2,1,0:T(2,128)(2,1)S(1)}, u32[]{:S(2)}, u32[]{:S(2)}) %collective-permute-start.11) | collective-permute-done | bytes 9248 | tf_op jit(solution)/shard_map/ppermute | solution.py:18
  117.3 3.6 %collective-permute-start.13 = (bf16[1,16,2,128]{3,2,1,0:T(2,128)(2,1)S(1)}, bf16[1,16,2,128]{3,2,1,0:T(2,128)(2,1)S(1)}, u32[]{:S(2)}, u32[]{:S(2)}) collective-permute-start(bf16[1,16,2,128]{3,2,1,0:T(2,128)(2,1)S(1)} %bitcast.376), channel_id=1, source_target_pairs={{8,0},{16,8},{24,16},{0,24},{9,1},{17,9},{25,17},{1,25},{10,2},{18... | collective-permute-start | bytes 24584 | tf_op jit(solution)/shard_map/ppermute | solution.py:18
  121.7 3.5 %collective-permute-done.12 = bf16[1,16,2,128]{3,2,1,0:T(2,128)(2,1)S(1)} collective-permute-done((bf16[1,16,2,128]{3,2,1,0:T(2,128)(2,1)S(1)}, bf16[1,16,2,128]{3,2,1,0:T(2,128)(2,1)S(1)}, u32[]{:S(2)}, u32[]{:S(2)}) %collective-permute-start.12) | collective-permute-done | bytes 8224 | tf_op jit(solution)/shard_map/ppermute | solution.py:17
  127.5 3.2 %collective-permute-done.15 = bf16[18,1,2,128]{3,2,1,0:T(2,128)(2,1)S(1)} collective-permute-done((bf16[18,1,2,128]{3,2,1,0:T(2,128)(2,1)S(1)}, bf16[18,1,2,128]{3,2,1,0:T(2,128)(2,1)S(1)}, u32[]{:S(2)}, u32[]{:S(2)}) %collective-permute-start.15) | collective-permute-done | bytes 9248 | tf_op jit(solution)/shard_map/ppermute | solution.py:18
  134.1 3.3 %collective-permute-start.17 = (bf16[1,32,2,256]{3,2,1,0:T(2,128)(2,1)S(1)}, bf16[1,32,2,256]{3,2,1,0:T(2,128)(2,1)S(1)}, u32[]{:S(2)}, u32[]{:S(2)}) collective-permute-start(bf16[1,32,2,256]{3,2,1,0:T(2,128)(2,1)S(1)} %get-tuple-element.17), channel_id=1, source_target_pairs={{8,0},{16,8},{24,16},{0,24},{9,1},{17,9},{25,17},{1,25},{10,2},{18... | collective-permute-start | bytes 98312 | tf_op jit(solution)/shard_map/ppermute | solution.py:18
  141.0 3.2 %collective-permute-done.19 = bf16[34,1,2,256]{3,2,1,0:T(2,128)(2,1)S(1)} collective-permute-done((bf16[34,1,2,256]{3,2,1,0:T(2,128)(2,1)S(1)}, bf16[34,1,2,256]{3,2,1,0:T(2,128)(2,1)S(1)}, u32[]{:S(2)}, u32[]{:S(2)}) %collective-permute-start.19) | collective-permute-done | bytes 34848 | tf_op jit(solution)/shard_map/ppermute | solution.py:18
  144.2 5.8 %broadcast_select_fusion = bf16[34,34,2,256]{3,2,1,0:T(2,128)(2,1)S(1)} fusion(pred[34]{0:T(512)(128)(4,1)S(1)} %compare_and_fusion.2, bf16[34,1,2,256]{3,2,1,0:T(2,128)(2,1)S(1)} %collective-permute-done.19, bf16[1,32,2,256]{3,2,1,0:T(2,128)(2,1)S(1)} %collective-permute-done.17, bf16[32,32,2,128]{3,2,1,0:T(2,128)(2,1)S(1)} %bitcast.305, ...), kind=kLoop, calls=%fused_computation.34 | loop fusion | flops 7694336 | bytes 2367522 | tf_op jit(solution)/shard_map/jit(_where)/select_n | solution.py:46
  150.0 10.8 %fusion.117 = (bf16[32,32,2,256]{3,2,1,0:T(2,128)(2,1)S(1)}, bf16[32,32,2,256]{3,2,1,0:T(2,128)(2,1)S(1)}, bf16[32,32,2,256]{3,2,1,0:T(2,128)(2,1)S(1)}, bf16[32...) fusion(bf16[34,34,2,256]{3,2,1,0:T(2,128)(2,1)S(1)} %broadcast_, ...), kind=kLoop, calls=%fused_computation.215 | loop fusion | bytes 18874368 | tf_op jit(solution)/shard_map/slice | solution.py:32
  166.5 2.3 %reshape.313 = bf16[2048,256]{1,0:T(8,128)(2,1)} reshape(bf16[32,32,2,256]{3,2,1,0:T(2,128)(2,1)} %get-tuple-element.10) | data formatting | bytes 2097152 | tf_op jit(solution)/shard_map/reshape | solution.py:32
  184.0 3.6 %collective-permute-start.21 = (bf16[1,32,2,128]{3,2,1,0:T(2,128)(2,1)S(1)}, bf16[1,32,2,128]{3,2,1,0:T(2,128)(2,1)S(1)}, u32[]{:S(2)}, u32[]{:S(2)}) collective-permute-start(bf16[1,32,2,128]{3,2,1,0:T(2,128)(2,1)S(1)} %bitcast.374), channel_id=1, source_target_pairs={{8,0},{16,8},{24,16},{0,24},{9,1},{17,9},{25,17},{1,25},{10,2},{18... | collective-permute-start | bytes 49160 | tf_op jit(solution)/shard_map/ppermute | solution.py:18
  188.5 3.5 %collective-permute-done.20 = bf16[1,32,2,128]{3,2,1,0:T(2,128)(2,1)S(1)} collective-permute-done((bf16[1,32,2,128]{3,2,1,0:T(2,128)(2,1)S(1)}, bf16[1,32,2,128]{3,2,1,0:T(2,128)(2,1)S(1)}, u32[]{:S(2)}, u32[]{:S(2)}) %collective-permute-start.20) | collective-permute-done | bytes 16416 | tf_op jit(solution)/shard_map/ppermute | solution.py:17
  194.4 3.2 %collective-permute-done.23 = bf16[34,1,2,128]{3,2,1,0:T(2,128)(2,1)S(1)} collective-permute-done((bf16[34,1,2,128]{3,2,1,0:T(2,128)(2,1)S(1)}, bf16[34,1,2,128]{3,2,1,0:T(2,128)(2,1)S(1)}, u32[]{:S(2)}, u32[]{:S(2)}) %collective-permute-start.23) | collective-permute-done | bytes 17440 | tf_op jit(solution)/shard_map/ppermute | solution.py:18
  199.4 5.2 %fusion.118 = (bf16[32,32,2,128]{3,2,1,0:T(2,128)(2,1)S(1)}, bf16[32,32,2,128]{3,2,1,0:T(2,128)(2,1)S(1)}, bf16[32,32,2,128]{3,2,1,0:T(2,128)(2,1)S(1)}, bf16[32...) fusion(bf16[34,34,2,128]{3,2,1,0:T(2,128)(2,1)S(1)} %broadcast_, ...), kind=kLoop, calls=%fused_computation.216 | loop fusion | bytes 9437184 | tf_op jit(solution)/shard_map/slice | solution.py:32
  (170 shorter events, 70.8 us)
Async XLA Ops:
  6.5 32.3 %all-gather.2.cloned.1.call-start = ((), (), s32[]{:S(2)}) async-start(), calls=%async_computation | async-start | bytes 2359296 | tf_op jit(solution)/shard_map/all_gather | solution.py:72
  60.5 4.4 %collective-permute-start = (bf16[1,32,2,64]{3,2,1,0:T(2,128)(2,1)S(1)}, bf16[1,32,2,64]{3,2,1,0:T(2,128)(2,1)S(1)}, u32[]{:S(2)}, u32[]{:S(2)}) collective-permute-start(bf16[1,32,2,64]{3,2,1,0:T(2,128)(2,1)S(1)} %slice.421), channel_id=1, source_target_pairs={{0,8},{8,16},{16,24},{24,0},{1,9},{9,17},{17,25},{25,1},{2,10},{10... | collective-permute-start | bytes 24584 | tf_op jit(solution)/shard_map/ppermute | solution.py:17
  62.0 3.4 %collective-permute-start.1 = (bf16[1,32,2,64]{3,2,1,0:T(2,128)(2,1)S(1)}, bf16[1,32,2,64]{3,2,1,0:T(2,128)(2,1)S(1)}, u32[]{:S(2)}, u32[]{:S(2)}) collective-permute-start(bf16[1,32,2,64]{3,2,1,0:T(2,128)(2,1)S(1)} %slice.423), channel_id=1, source_target_pairs={{8,0},{16,8},{24,16},{0,24},{9,1},{17,9},{25,17},{1,25},{10,2},{18... | collective-permute-start | bytes 24584 | tf_op jit(solution)/shard_map/ppermute | solution.py:18
  65.5 3.5 %collective-permute-start.2 = (bf16[34,1,2,64]{3,2,1,0:T(2,128)(2,1)S(1)}, bf16[34,1,2,64]{3,2,1,0:T(2,128)(2,1)S(1)}, u32[]{:S(2)}, u32[]{:S(2)}) collective-permute-start(bf16[34,1,2,64]{3,2,1,0:T(2,128)(2,1)S(1)} %get-tuple-element.49), channel_id=1, source_target_pairs={{0,1},{1,2},{2,3},{3,4},{4,5},{5,6},{6,7},{7,0},{8,9},{9,10},{10,1... | collective-permute-start | bytes 26120 | tf_op jit(solution)/shard_map/ppermute | solution.py:17
  68.1 4.1 %collective-permute-start.3 = (bf16[34,1,2,64]{3,2,1,0:T(2,128)(2,1)S(1)}, bf16[34,1,2,64]{3,2,1,0:T(2,128)(2,1)S(1)}, u32[]{:S(2)}, u32[]{:S(2)}) collective-permute-start(bf16[34,1,2,64]{3,2,1,0:T(2,128)(2,1)S(1)} %get-tuple-element.50), channel_id=1, source_target_pairs={{1,0},{2,1},{3,2},{4,3},{5,4},{6,5},{7,6},{0,7},{9,8},{10,9},{11,1... | collective-permute-start | bytes 26120 | tf_op jit(solution)/shard_map/ppermute | solution.py:18
  81.2 4.0 %collective-permute-start.5 = (bf16[1,32,2,128]{3,2,1,0:T(2,128)(2,1)S(1)}, bf16[1,32,2,128]{3,2,1,0:T(2,128)(2,1)S(1)}, u32[]{:S(2)}, u32[]{:S(2)}) collective-permute-start(bf16[1,32,2,128]{3,2,1,0:T(2,128)(2,1)S(1)} %bitcast.373), channel_id=1, source_target_pairs={{8,0},{16,8},{24,16},{0,24},{9,1},{17,9},{25,17},{1,25},{10,2},{18... | collective-permute-start | bytes 49160 | tf_op jit(solution)/shard_map/ppermute | solution.py:18
  84.4 4.4 %collective-permute-start.4 = (bf16[1,32,2,128]{3,2,1,0:T(2,128)(2,1)S(1)}, bf16[1,32,2,128]{3,2,1,0:T(2,128)(2,1)S(1)}, u32[]{:S(2)}, u32[]{:S(2)}) collective-permute-start(bf16[1,32,2,128]{3,2,1,0:T(2,128)(2,1)S(1)} %bitcast.371), channel_id=1, source_target_pairs={{0,8},{8,16},{16,24},{24,0},{1,9},{9,17},{17,25},{25,1},{2,10},{10... | collective-permute-start | bytes 49160 | tf_op jit(solution)/shard_map/ppermute | solution.py:17
  88.8 2.4 %collective-permute-start.6 = (bf16[34,1,2,128]{3,2,1,0:T(2,128)(2,1)S(1)}, bf16[34,1,2,128]{3,2,1,0:T(2,128)(2,1)S(1)}, u32[]{:S(2)}, u32[]{:S(2)}) collective-permute-start(bf16[34,1,2,128]{3,2,1,0:T(2,128)(2,1)S(1)} %get-tuple-element.47), channel_id=1, source_target_pairs={{0,1},{1,2},{2,3},{3,4},{4,5},{5,6},{6,7},{7,0},{8,9},{9,10},{10,1... | collective-permute-start | bytes 52232 | tf_op jit(solution)/shard_map/ppermute | solution.py:17
  90.4 4.1 %collective-permute-start.7 = (bf16[34,1,2,128]{3,2,1,0:T(2,128)(2,1)S(1)}, bf16[34,1,2,128]{3,2,1,0:T(2,128)(2,1)S(1)}, u32[]{:S(2)}, u32[]{:S(2)}) collective-permute-start(bf16[34,1,2,128]{3,2,1,0:T(2,128)(2,1)S(1)} %get-tuple-element.48), channel_id=1, source_target_pairs={{1,0},{2,1},{3,2},{4,3},{5,4},{6,5},{7,6},{0,7},{9,8},{10,9},{11,1... | collective-permute-start | bytes 52232 | tf_op jit(solution)/shard_map/ppermute | solution.py:18
  104.9 4.4 %collective-permute-start.8 = (bf16[1,16,2,128]{3,2,1,0:T(2,128)(2,1)S(1)}, bf16[1,16,2,128]{3,2,1,0:T(2,128)(2,1)S(1)}, u32[]{:S(2)}, u32[]{:S(2)}) collective-permute-start(bf16[1,16,2,128]{3,2,1,0:T(2,128)(2,1)S(1)} %get-tuple-element.81), channel_id=1, source_target_pairs={{0,8},{8,16},{16,24},{24,0},{1,9},{9,17},{17,25},{25,1},{2,10},{10... | collective-permute-start | bytes 24584 | tf_op jit(solution)/shard_map/ppermute | solution.py:17
  104.9 4.3 %collective-permute-start.9 = (bf16[1,16,2,128]{3,2,1,0:T(2,128)(2,1)S(1)}, bf16[1,16,2,128]{3,2,1,0:T(2,128)(2,1)S(1)}, u32[]{:S(2)}, u32[]{:S(2)}) collective-permute-start(bf16[1,16,2,128]{3,2,1,0:T(2,128)(2,1)S(1)} %get-tuple-element.82), channel_id=1, source_target_pairs={{8,0},{16,8},{24,16},{0,24},{9,1},{17,9},{25,17},{1,25},{10,2},{18... | collective-permute-start | bytes 24584 | tf_op jit(solution)/shard_map/ppermute | solution.py:18
  110.6 4.0 %collective-permute-start.11 = (bf16[18,1,2,128]{3,2,1,0:T(2,128)(2,1)S(1)}, bf16[18,1,2,128]{3,2,1,0:T(2,128)(2,1)S(1)}, u32[]{:S(2)}, u32[]{:S(2)}) collective-permute-start(bf16[18,1,2,128]{3,2,1,0:T(2,128)(2,1)S(1)} %get-tuple-element.78), channel_id=1, source_target_pairs={{1,0},{2,1},{3,2},{4,3},{5,4},{6,5},{7,6},{0,7},{9,8},{10,9},{11,1... | collective-permute-start | bytes 27656 | tf_op jit(solution)/shard_map/ppermute | solution.py:18
  117.3 4.4 %collective-permute-start.13 = (bf16[1,16,2,128]{3,2,1,0:T(2,128)(2,1)S(1)}, bf16[1,16,2,128]{3,2,1,0:T(2,128)(2,1)S(1)}, u32[]{:S(2)}, u32[]{:S(2)}) collective-permute-start(bf16[1,16,2,128]{3,2,1,0:T(2,128)(2,1)S(1)} %bitcast.376), channel_id=1, source_target_pairs={{8,0},{16,8},{24,16},{0,24},{9,1},{17,9},{25,17},{1,25},{10,2},{18... | collective-permute-start | bytes 24584 | tf_op jit(solution)/shard_map/ppermute | solution.py:18
  120.9 4.3 %collective-permute-start.12 = (bf16[1,16,2,128]{3,2,1,0:T(2,128)(2,1)S(1)}, bf16[1,16,2,128]{3,2,1,0:T(2,128)(2,1)S(1)}, u32[]{:S(2)}, u32[]{:S(2)}) collective-permute-start(bf16[1,16,2,128]{3,2,1,0:T(2,128)(2,1)S(1)} %bitcast.375), channel_id=1, source_target_pairs={{0,8},{8,16},{16,24},{24,0},{1,9},{9,17},{17,25},{25,1},{2,10},{10... | collective-permute-start | bytes 24584 | tf_op jit(solution)/shard_map/ppermute | solution.py:17
  125.2 2.3 %collective-permute-start.14 = (bf16[18,1,2,128]{3,2,1,0:T(2,128)(2,1)S(1)}, bf16[18,1,2,128]{3,2,1,0:T(2,128)(2,1)S(1)}, u32[]{:S(2)}, u32[]{:S(2)}) collective-permute-start(bf16[18,1,2,128]{3,2,1,0:T(2,128)(2,1)S(1)} %get-tuple-element.75), channel_id=1, source_target_pairs={{0,1},{1,2},{2,3},{3,4},{4,5},{5,6},{6,7},{7,0},{8,9},{9,10},{10,1... | collective-permute-start | bytes 27656 | tf_op jit(solution)/shard_map/ppermute | solution.py:17
  126.7 4.0 %collective-permute-start.15 = (bf16[18,1,2,128]{3,2,1,0:T(2,128)(2,1)S(1)}, bf16[18,1,2,128]{3,2,1,0:T(2,128)(2,1)S(1)}, u32[]{:S(2)}, u32[]{:S(2)}) collective-permute-start(bf16[18,1,2,128]{3,2,1,0:T(2,128)(2,1)S(1)} %get-tuple-element.76), channel_id=1, source_target_pairs={{1,0},{2,1},{3,2},{4,3},{5,4},{6,5},{7,6},{0,7},{9,8},{10,9},{11,1... | collective-permute-start | bytes 27656 | tf_op jit(solution)/shard_map/ppermute | solution.py:18
  134.0 4.6 %collective-permute-start.16 = (bf16[1,32,2,256]{3,2,1,0:T(2,128)(2,1)S(1)}, bf16[1,32,2,256]{3,2,1,0:T(2,128)(2,1)S(1)}, u32[]{:S(2)}, u32[]{:S(2)}) collective-permute-start(bf16[1,32,2,256]{3,2,1,0:T(2,128)(2,1)S(1)} %get-tuple-element.16), channel_id=1, source_target_pairs={{0,8},{8,16},{16,24},{24,0},{1,9},{9,17},{17,25},{25,1},{2,10},{10... | collective-permute-start | bytes 98312 | tf_op jit(solution)/shard_map/ppermute | solution.py:17
  134.1 4.6 %collective-permute-start.17 = (bf16[1,32,2,256]{3,2,1,0:T(2,128)(2,1)S(1)}, bf16[1,32,2,256]{3,2,1,0:T(2,128)(2,1)S(1)}, u32[]{:S(2)}, u32[]{:S(2)}) collective-permute-start(bf16[1,32,2,256]{3,2,1,0:T(2,128)(2,1)S(1)} %get-tuple-element.17), channel_id=1, source_target_pairs={{8,0},{16,8},{24,16},{0,24},{9,1},{17,9},{25,17},{1,25},{10,2},{18... | collective-permute-start | bytes 98312 | tf_op jit(solution)/shard_map/ppermute | solution.py:18
  138.7 2.3 %collective-permute-start.18 = (bf16[34,1,2,256]{3,2,1,0:T(2,128)(2,1)S(1)}, bf16[34,1,2,256]{3,2,1,0:T(2,128)(2,1)S(1)}, u32[]{:S(2)}, u32[]{:S(2)}) collective-permute-start(bf16[34,1,2,256]{3,2,1,0:T(2,128)(2,1)S(1)} %get-tuple-element.14), channel_id=1, source_target_pairs={{0,1},{1,2},{2,3},{3,4},{4,5},{5,6},{6,7},{7,0},{8,9},{9,10},{10,1... | collective-permute-start | bytes 104456 | tf_op jit(solution)/shard_map/ppermute | solution.py:17
  139.9 4.3 %collective-permute-start.19 = (bf16[34,1,2,256]{3,2,1,0:T(2,128)(2,1)S(1)}, bf16[34,1,2,256]{3,2,1,0:T(2,128)(2,1)S(1)}, u32[]{:S(2)}, u32[]{:S(2)}) collective-permute-start(bf16[34,1,2,256]{3,2,1,0:T(2,128)(2,1)S(1)} %get-tuple-element.15), channel_id=1, source_target_pairs={{1,0},{2,1},{3,2},{4,3},{5,4},{6,5},{7,6},{0,7},{9,8},{10,9},{11,1... | collective-permute-start | bytes 104456 | tf_op jit(solution)/shard_map/ppermute | solution.py:18
  184.0 4.5 %collective-permute-start.21 = (bf16[1,32,2,128]{3,2,1,0:T(2,128)(2,1)S(1)}, bf16[1,32,2,128]{3,2,1,0:T(2,128)(2,1)S(1)}, u32[]{:S(2)}, u32[]{:S(2)}) collective-permute-start(bf16[1,32,2,128]{3,2,1,0:T(2,128)(2,1)S(1)} %bitcast.374), channel_id=1, source_target_pairs={{8,0},{16,8},{24,16},{0,24},{9,1},{17,9},{25,17},{1,25},{10,2},{18... | collective-permute-start | bytes 49160 | tf_op jit(solution)/shard_map/ppermute | solution.py:18
  187.6 4.4 %collective-permute-start.20 = (bf16[1,32,2,128]{3,2,1,0:T(2,128)(2,1)S(1)}, bf16[1,32,2,128]{3,2,1,0:T(2,128)(2,1)S(1)}, u32[]{:S(2)}, u32[]{:S(2)}) collective-permute-start(bf16[1,32,2,128]{3,2,1,0:T(2,128)(2,1)S(1)} %bitcast.372), channel_id=1, source_target_pairs={{0,8},{8,16},{16,24},{24,0},{1,9},{9,17},{17,25},{25,1},{2,10},{10... | collective-permute-start | bytes 49160 | tf_op jit(solution)/shard_map/ppermute | solution.py:17
  192.1 2.4 %collective-permute-start.22 = (bf16[34,1,2,128]{3,2,1,0:T(2,128)(2,1)S(1)}, bf16[34,1,2,128]{3,2,1,0:T(2,128)(2,1)S(1)}, u32[]{:S(2)}, u32[]{:S(2)}) collective-permute-start(bf16[34,1,2,128]{3,2,1,0:T(2,128)(2,1)S(1)} %get-tuple-element.45), channel_id=1, source_target_pairs={{0,1},{1,2},{2,3},{3,4},{4,5},{5,6},{6,7},{7,0},{8,9},{9,10},{10,1... | collective-permute-start | bytes 52232 | tf_op jit(solution)/shard_map/ppermute | solution.py:17
  193.6 4.1 %collective-permute-start.23 = (bf16[34,1,2,128]{3,2,1,0:T(2,128)(2,1)S(1)}, bf16[34,1,2,128]{3,2,1,0:T(2,128)(2,1)S(1)}, u32[]{:S(2)}, u32[]{:S(2)}) collective-permute-start(bf16[34,1,2,128]{3,2,1,0:T(2,128)(2,1)S(1)} %get-tuple-element.46), channel_id=1, source_target_pairs={{1,0},{2,1},{3,2},{4,3},{5,4},{6,5},{7,6},{0,7},{9,8},{10,9},{11,1... | collective-permute-start | bytes 52232 | tf_op jit(solution)/shard_map/ppermute | solution.py:18
  (13 other events, 253.5 us)
Sparse Core Ops, SparseCore 0:
  9.2 29.5 all-gather.1
where the time goes:
time: 216 us
  local copies, waits for them, and re-layouts  71.4 us (33%)
  waiting for transfers between devices  68.8 us (32%)
  starting transfers between devices  30 us (14%)
  matrix products  16.6 us (8%)
  other arithmetic  14.8 us (7%)
  between operations  14.2 us (7%)
    slice x6, local copies, waits for them, and re-layouts, conv_valid(): padded[row_step:row_step + height, col_step:col_step + width]  27.9 us
    all_gather x1, waiting for transfers between devices, body(): lax.all_gather(source_tiles, 'col', axis=1, tiled=True).reshape(-1, columns)  27.5 us
    ppermute x12, waiting for transfers between devices, with_halo(): after = lax.ppermute(leading, axis, down)  21.7 us
    ppermute x12, starting transfers between devices, with_halo(): after = lax.ppermute(leading, axis, down)  18.9 us
    ppermute x12, waiting for transfers between devices, with_halo(): before = lax.ppermute(last, axis, up)  18.9 us
    dot_general x54, matrix products, conv_valid(): jnp.dot(window, weight[row_step, col_step], preferred_element_type=jnp.fl...  16.3 us
    reshape x9, local copies, waits for them, and re-layouts, conv_valid(): padded[row_step:row_step + height, col_step:col_step + width]  14.8 us
    gather x1, local copies, waits for them, and re-layouts, body(): picked = buffer[stencil]  12.1 us
  transfers between devices with their start and end apart: 25, of which 22 were waited for; matrix products, arithmetic and copies ran while one was open for 2% of the time, Pallas kernels for 0%

commit v1 on v0

--- a/solution.py
+++ b/solution.py
@@ -5,6 +5,19 @@
 
 FIELDS = 64
 CH = 128
+
+
+def collect(shard, axis, dim):
+    ways = lax.axis_size(axis)
+    up = [(d, (d + 1) % ways) for d in range(ways)]
+    down = [(d, (d - 1) % ways) for d in range(ways)]
+    earlier, later = ([shard], [shard])
+    for _ in range(ways // 2):
+        earlier.append(lax.ppermute(earlier[-1], axis, up))
+    for _ in range((ways - 1) // 2):
+        later.append(lax.ppermute(later[-1], axis, down))
+    line = jnp.concatenate([*earlier[::-1], *later[1:]], axis=dim)
+    return jnp.roll(line, (lax.axis_index(axis) - ways // 2) * shard.shape[dim], axis=dim)
 
 
 def with_halo(x, sides, width):
@@ -69,7 +82,7 @@
     wanted = requests.reshape(groups, capacity)
     global_ids = (jnp.arange(groups, dtype=jnp.int32)[:, None] * cells + wanted).reshape(-1)
     empty = jnp.zeros((groups * capacity, columns), jnp.bfloat16)
-    flattened = lax.all_gather(source_tiles, "col", axis=1, tiled=True).reshape(-1, columns)
+    flattened = collect(source_tiles, "col", 1).reshape(-1, columns)
     inside = (global_ids >= 0) & (global_ids < flattened.shape[0])
     picked = flattened[jnp.clip(global_ids, 0, flattened.shape[0] - 1)]
     buffer = jnp.where(inside[:, None], picked, empty)

time: 216 us -> 192 us (0.89)
  waiting for transfers between devices: 68.8 us -> 46.7 us
  starting transfers between devices: 30 us -> 43.8 us
  between operations: 14.2 us -> 1 us
  local copies, waits for them, and re-layouts: 71.4 us -> 67.7 us
    all_gather x1 -> x0, waiting for transfers between devices: 27.5 us -> none  [body(): lax.all_gather(source_tiles, 'col', axis=1, tiled=True).reshape(-1, columns)]
    ppermute x0 -> x7, waiting for transfers between devices: none -> 18.7 us  [the longest x4 15.8 us: collect(): earlier.append(lax.ppermute(earlier[-1], axis, up))]
    ppermute x0 -> x7, starting transfers between devices: none -> 11.9 us  [the longest x4 11.8 us: collect(): earlier.append(lax.ppermute(earlier[-1], axis, up))]
    ppermute x12, waiting for transfers between devices: 18.9 us -> 10.6 us  [with_halo(): before = lax.ppermute(last, axis, up)]
    ppermute x12, waiting for transfers between devices: 21.7 us -> 17.4 us  [with_halo(): after = lax.ppermute(leading, axis, down)]
    ppermute x12, starting transfers between devices: 11.1 us -> 14.5 us  [with_halo(): before = lax.ppermute(last, axis, up)]
    unnamed x32 -> x47, local copies, waits for them, and re-layouts: 6.32 us -> 3.71 us
  transfers between devices with their start and end apart: 25 -> 31, of which waited for: 22 -> 22; matrix products, arithmetic and copies ran while one was open for 2% -> 3% of each run, Pallas kernels for 0% -> 0%
where the time goes in v1:
time: 192 us
  local copies, waits for them, and re-layouts  67.7 us (35%)
  waiting for transfers between devices  46.7 us (24%)
  starting transfers between devices  43.8 us (23%)
  matrix products  17.9 us (9%)
  other arithmetic  14.8 us (8%)
    slice x6, local copies, waits for them, and re-layouts, conv_valid(): padded[row_step:row_step + height, col_step:col_step + width]  27.9 us
    dot_general x54, matrix products, conv_valid(): jnp.dot(window, weight[row_step, col_step], preferred_element_type=jnp.fl...  17.6 us
    ppermute x12, waiting for transfers between devices, with_halo(): after = lax.ppermute(leading, axis, down)  17.4 us
    ppermute x12, starting transfers between devices, with_halo(): after = lax.ppermute(leading, axis, down)  17.4 us
    ppermute x4, waiting for transfers between devices, collect(): earlier.append(lax.ppermute(earlier[-1], axis, up))  15.8 us
    reshape x9, local copies, waits for them, and re-layouts, conv_valid(): padded[row_step:row_step + height, col_step:col_step + width]  14.8 us
    ppermute x12, starting transfers between devices, with_halo(): before = lax.ppermute(last, axis, up)  14.5 us
    gather x1, local copies, waits for them, and re-layouts, body(): picked = buffer[stencil]  12.1 us
  transfers between devices with their start and end apart: 31, of which 22 were waited for; matrix products, arithmetic and copies ran while one was open for 3% of the time, Pallas kernels for 0%

profile of v1, /device:TPU:3, one launch (start us, length us, event | category | flops | bytes accessed | tf_op | source)
XLA Modules:
  0.0 191.8 jit_solution(14603352234749171055)
XLA Ops:
  3.3 4.1 %collective-permute-done = bf16[1,1,1024,128]{3,2,1,0:T(8,128)(2,1)S(1)} collective-permute-done((bf16[1,1,1024,128]{3,2,1,0:T(8,128)(2,1)}, bf16[1,1,1024,128]{3,2,1,0:T(8,128)(2,1)S(1)}, u32[]{:S(2)}, u32[]{:S(2)}) %collective-permute-start) | collective-permute-done | bytes 262176 | tf_op jit(solution)/shard_map/ppermute | solution.py:16
  7.4 3.3 %collective-permute-start.1 = (bf16[1,1,1024,128]{3,2,1,0:T(8,128)(2,1)S(1)}, bf16[1,1,1024,128]{3,2,1,0:T(8,128)(2,1)S(1)}, u32[]{:S(2)}, u32[]{:S(2)}) collective-permute-start(bf16[1,1,1024,128]{3,2,1,0:T(8,128)(2,1)S(1)} %collective-permute-done), channel_id=1, source_target_pairs={{0,1},{1,2},{2,3},{3,4},{4,5},{5,6},{6,7},{7,0},{8,9},{9,10},{10,1... | collective-permute-start | bytes 786440 | tf_op jit(solution)/shard_map/ppermute | solution.py:16
  10.7 3.3 %collective-permute-done.1 = bf16[1,1,1024,128]{3,2,1,0:T(8,128)(2,1)S(1)} collective-permute-done((bf16[1,1,1024,128]{3,2,1,0:T(8,128)(2,1)S(1)}, bf16[1,1,1024,128]{3,2,1,0:T(8,128)(2,1)S(1)}, u32[]{:S(2)}, u32[]{:S(2)}) %collective-permute-start.1) | collective-permute-done | bytes 262176 | tf_op jit(solution)/shard_map/ppermute | solution.py:16
  14.0 3.4 %collective-permute-start.2 = (bf16[1,1,1024,128]{3,2,1,0:T(8,128)(2,1)S(1)}, bf16[1,1,1024,128]{3,2,1,0:T(8,128)(2,1)S(1)}, u32[]{:S(2)}, u32[]{:S(2)}) collective-permute-start(bf16[1,1,1024,128]{3,2,1,0:T(8,128)(2,1)S(1)} %collective-permute-done.1), channel_id=1, source_target_pairs={{0,1},{1,2},{2,3},{3,4},{4,5},{5,6},{6,7},{7,0},{8,9},{9,10},{10,1... | collective-permute-start | bytes 786440 | tf_op jit(solution)/shard_map/ppermute | solution.py:16
  18.3 4.9 %collective-permute-done.2 = bf16[1,1,1024,128]{3,2,1,0:T(8,128)(2,1)S(1)} collective-permute-done((bf16[1,1,1024,128]{3,2,1,0:T(8,128)(2,1)S(1)}, bf16[1,1,1024,128]{3,2,1,0:T(8,128)(2,1)S(1)}, u32[]{:S(2)}, u32[]{:S(2)}) %collective-permute-start.2) | collective-permute-done | bytes 262176 | tf_op jit(solution)/shard_map/ppermute | solution.py:16
  23.2 3.4 %collective-permute-start.3 = (bf16[1,1,1024,128]{3,2,1,0:T(8,128)(2,1)S(1)}, bf16[1,1,1024,128]{3,2,1,0:T(8,128)(2,1)S(1)}, u32[]{:S(2)}, u32[]{:S(2)}) collective-permute-start(bf16[1,1,1024,128]{3,2,1,0:T(8,128)(2,1)S(1)} %collective-permute-done.2), channel_id=1, source_target_pairs={{0,1},{1,2},{2,3},{3,4},{4,5},{5,6},{6,7},{7,0},{8,9},{9,10},{10,1... | collective-permute-start | bytes 786440 | tf_op jit(solution)/shard_map/ppermute | solution.py:16
  28.4 3.5 %collective-permute-done.3 = bf16[1,1,1024,128]{3,2,1,0:T(8,128)(2,1)S(1)} collective-permute-done((bf16[1,1,1024,128]{3,2,1,0:T(8,128)(2,1)S(1)}, bf16[1,1,1024,128]{3,2,1,0:T(8,128)(2,1)S(1)}, u32[]{:S(2)}, u32[]{:S(2)}) %collective-permute-start.3) | collective-permute-done | bytes 262176 | tf_op jit(solution)/shard_map/ppermute | solution.py:16
  32.2 2.9 %collective-permute-done.6 = bf16[1,1,1024,128]{3,2,1,0:T(8,128)(2,1)S(1)} collective-permute-done((bf16[1,1,1024,128]{3,2,1,0:T(8,128)(2,1)S(1)}, bf16[1,1,1024,128]{3,2,1,0:T(8,128)(2,1)S(1)}, u32[]{:S(2)}, u32[]{:S(2)}) %collective-permute-start.6) | collective-permute-done | bytes 262176 | tf_op jit(solution)/shard_map/ppermute | solution.py:18
  35.6 6.2 %gather_fusion = bf16[2048,128]{1,0:T(8,128)(2,1)S(1)} fusion(bf16[8192,128]{1,0:T(8,128)(2,1)S(1)} %bitcast.300, s32[2048]{0:T(1024)S(1)} %broadcast_clamp_fusion.1), kind=kCustom, calls=%fused_computation | custom fusion | bytes 1056768 | tf_op jit(solution)/shard_map/gather | solution.py:87
  42.1 12.1 %gather_fusion.1 = bf16[4096,128]{1,0:T(8,128)(2,1)S(1)} fusion(bf16[2048,128]{1,0:T(8,128)(2,1)S(1)} %broadcast_select_fusion.4, s32[4096]{0:T(1024)S(1)} %broadcast_clamp_fusion), kind=kCustom, calls=%fused_computation.1 | custom fusion | bytes 2113536 | tf_op jit(solution)/shard_map/gather | solution.py:89
  66.2 5.2 %fusion.120 = (bf16[32,32,2,64]{3,2,1,0:T(2,128)(2,1)S(1)}, bf16[32,32,2,64]{3,2,1,0:T(2,128)(2,1)S(1)}, bf16[32,32,2,64]{3,2,1,0:T(2,128)(2,1)S(1)}, bf16[32,32...) fusion(bf16[34,34,2,64]{3,2,1,0:T(2,128)(2,1)S(1)} %broadcast_s, ...), kind=kLoop, calls=%fused_computation.235 | loop fusion | bytes 4718592 | tf_op jit(solution)/shard_map/slice | solution.py:45
  74.2 3.3 %collective-permute-start.12 = (bf16[1,32,2,128]{3,2,1,0:T(2,128)(2,1)S(1)}, bf16[1,32,2,128]{3,2,1,0:T(2,128)(2,1)S(1)}, u32[]{:S(2)}, u32[]{:S(2)}) collective-permute-start(bf16[1,32,2,128]{3,2,1,0:T(2,128)(2,1)S(1)} %bitcast.369), channel_id=1, source_target_pairs={{8,0},{16,8},{24,16},{0,24},{9,1},{17,9},{25,17},{1,25},{10,2},{18... | collective-permute-start | bytes 49160 | tf_op jit(solution)/shard_map/ppermute | solution.py:31
  78.6 3.8 %collective-permute-start.13 = (bf16[34,1,2,128]{3,2,1,0:T(2,128)(2,1)S(1)}, bf16[34,1,2,128]{3,2,1,0:T(2,128)(2,1)S(1)}, u32[]{:S(2)}, u32[]{:S(2)}) collective-permute-start(bf16[34,1,2,128]{3,2,1,0:T(2,128)(2,1)S(1)} %get-tuple-element.47), channel_id=1, source_target_pairs={{0,1},{1,2},{2,3},{3,4},{4,5},{5,6},{6,7},{7,0},{8,9},{9,10},{10,1... | collective-permute-start | bytes 52232 | tf_op jit(solution)/shard_map/ppermute | solution.py:30
  83.3 3.2 %collective-permute-done.14 = bf16[34,1,2,128]{3,2,1,0:T(2,128)(2,1)S(1)} collective-permute-done((bf16[34,1,2,128]{3,2,1,0:T(2,128)(2,1)S(1)}, bf16[34,1,2,128]{3,2,1,0:T(2,128)(2,1)S(1)}, u32[]{:S(2)}, u32[]{:S(2)}) %collective-permute-start.14) | collective-permute-done | bytes 17440 | tf_op jit(solution)/shard_map/ppermute | solution.py:31
  88.3 5.2 %fusion.119 = (bf16[32,32,2,128]{3,2,1,0:T(2,128)(2,1)S(1)}, bf16[32,32,2,128]{3,2,1,0:T(2,128)(2,1)S(1)}, bf16[32,32,2,128]{3,2,1,0:T(2,128)(2,1)S(1)}, bf16[32...) fusion(bf16[34,34,2,128]{3,2,1,0:T(2,128)(2,1)S(1)} %broadcast_, ...), kind=kLoop, calls=%fused_computation.234 | loop fusion | bytes 9437184 | tf_op jit(solution)/shard_map/slice | solution.py:45
  97.5 3.2 %collective-permute-start.16 = (bf16[1,16,2,128]{3,2,1,0:T(2,128)(2,1)S(1)}, bf16[1,16,2,128]{3,2,1,0:T(2,128)(2,1)S(1)}, u32[]{:S(2)}, u32[]{:S(2)}) collective-permute-start(bf16[1,16,2,128]{3,2,1,0:T(2,128)(2,1)S(1)} %get-tuple-element.82), channel_id=1, source_target_pairs={{8,0},{16,8},{24,16},{0,24},{9,1},{17,9},{25,17},{1,25},{10,2},{18... | collective-permute-start | bytes 24584 | tf_op jit(solution)/shard_map/ppermute | solution.py:31
  103.4 3.2 %collective-permute-done.18 = bf16[18,1,2,128]{3,2,1,0:T(2,128)(2,1)S(1)} collective-permute-done((bf16[18,1,2,128]{3,2,1,0:T(2,128)(2,1)S(1)}, bf16[18,1,2,128]{3,2,1,0:T(2,128)(2,1)S(1)}, u32[]{:S(2)}, u32[]{:S(2)}) %collective-permute-start.18) | collective-permute-done | bytes 9248 | tf_op jit(solution)/shard_map/ppermute | solution.py:31
  110.2 2.8 %collective-permute-start.20 = (bf16[1,16,2,128]{3,2,1,0:T(2,128)(2,1)S(1)}, bf16[1,16,2,128]{3,2,1,0:T(2,128)(2,1)S(1)}, u32[]{:S(2)}, u32[]{:S(2)}) collective-permute-start(bf16[1,16,2,128]{3,2,1,0:T(2,128)(2,1)S(1)} %bitcast.373), channel_id=1, source_target_pairs={{8,0},{16,8},{24,16},{0,24},{9,1},{17,9},{25,17},{1,25},{10,2},{18... | collective-permute-start | bytes 24584 | tf_op jit(solution)/shard_map/ppermute | solution.py:31
  115.8 3.2 %collective-permute-done.22 = bf16[18,1,2,128]{3,2,1,0:T(2,128)(2,1)S(1)} collective-permute-done((bf16[18,1,2,128]{3,2,1,0:T(2,128)(2,1)S(1)}, bf16[18,1,2,128]{3,2,1,0:T(2,128)(2,1)S(1)}, u32[]{:S(2)}, u32[]{:S(2)}) %collective-permute-start.22) | collective-permute-done | bytes 9248 | tf_op jit(solution)/shard_map/ppermute | solution.py:31
  129.3 3.2 %collective-permute-done.26 = bf16[34,1,2,256]{3,2,1,0:T(2,128)(2,1)S(1)} collective-permute-done((bf16[34,1,2,256]{3,2,1,0:T(2,128)(2,1)S(1)}, bf16[34,1,2,256]{3,2,1,0:T(2,128)(2,1)S(1)}, u32[]{:S(2)}, u32[]{:S(2)}) %collective-permute-start.26) | collective-permute-done | bytes 34848 | tf_op jit(solution)/shard_map/ppermute | solution.py:31
  132.5 5.8 %broadcast_select_fusion = bf16[34,34,2,256]{3,2,1,0:T(2,128)(2,1)S(1)} fusion(pred[34]{0:T(512)(128)(4,1)S(1)} %compare_and_fusion.2, bf16[34,1,2,256]{3,2,1,0:T(2,128)(2,1)S(1)} %collective-permute-done.26, bf16[1,32,2,256]{3,2,1,0:T(2,128)(2,1)S(1)} %collective-permute-done.24, bf16[32,32,2,128]{3,2,1,0:T(2,128)(2,1)S(1)} %bitcast.304, ...), kind=kLoop, calls=%fused_computation.34 | loop fusion | flops 7694336 | bytes 2367522 | tf_op jit(solution)/shard_map/jit(_where)/select_n | solution.py:59
  138.3 10.7 %fusion.117 = (bf16[32,32,2,256]{3,2,1,0:T(2,128)(2,1)}, bf16[32,32,2,256]{3,2,1,0:T(2,128)(2,1)}, bf16[32,32,2,256]{3,2,1,0:T(2,128)(2,1)S(1)}, bf16[32,32,2,25...) fusion(bf16[34,34,2,256]{3,2,1,0:T(2,128)(2,1)S(1)} %broadcast_, ...), kind=kLoop, calls=%fused_computation.232 | loop fusion | bytes 18874368 | tf_op jit(solution)/shard_map/slice | solution.py:45
  177.3 3.2 %collective-permute-done.30 = bf16[34,1,2,128]{3,2,1,0:T(2,128)(2,1)S(1)} collective-permute-done((bf16[34,1,2,128]{3,2,1,0:T(2,128)(2,1)S(1)}, bf16[34,1,2,128]{3,2,1,0:T(2,128)(2,1)S(1)}, u32[]{:S(2)}, u32[]{:S(2)}) %collective-permute-start.30) | collective-permute-done | bytes 17440 | tf_op jit(solution)/shard_map/ppermute | solution.py:31
  182.2 5.2 %fusion.118 = (bf16[32,32,2,128]{3,2,1,0:T(2,128)(2,1)S(1)}, bf16[32,32,2,128]{3,2,1,0:T(2,128)(2,1)S(1)}, bf16[32,32,2,128]{3,2,1,0:T(2,128)(2,1)S(1)}, bf16[32...) fusion(bf16[34,34,2,128]{3,2,1,0:T(2,128)(2,1)S(1)} %broadcast_, ...), kind=kLoop, calls=%fused_computation.233 | loop fusion | bytes 9437184 | tf_op jit(solution)/shard_map/slice | solution.py:45
  (198 shorter events, 82.5 us)
Async XLA Ops:
  0.0 7.4 %collective-permute-start = (bf16[1,1,1024,128]{3,2,1,0:T(8,128)(2,1)}, bf16[1,1,1024,128]{3,2,1,0:T(8,128)(2,1)S(1)}, u32[]{:S(2)}, u32[]{:S(2)}) collective-permute-start(bf16[1,1,1024,128]{3,2,1,0:T(8,128)(2,1)} %param.11), channel_id=1, source_target_pairs={{0,1},{1,2},{2,3},{3,4},{4,5},{5,6},{6,7},{7,0},{8,9},{9,10},{10,1... | collective-permute-start | bytes 786440 | tf_op jit(solution)/shard_map/ppermute | solution.py:16
  1.8 16.5 %collective-permute-start.4 = (bf16[1,1,1024,128]{3,2,1,0:T(8,128)(2,1)}, bf16[1,1,1024,128]{3,2,1,0:T(8,128)(2,1)S(1)}, u32[]{:S(2)}, u32[]{:S(2)}) collective-permute-start(bf16[1,1,1024,128]{3,2,1,0:T(8,128)(2,1)} %param.11), channel_id=1, source_target_pairs={{0,7},{1,0},{2,1},{3,2},{4,3},{5,4},{6,5},{7,6},{8,15},{9,8},{10,9... | collective-permute-start | bytes 786440 | tf_op jit(solution)/shard_map/ppermute | solution.py:18
  7.4 6.6 %collective-permute-start.1 = (bf16[1,1,1024,128]{3,2,1,0:T(8,128)(2,1)S(1)}, bf16[1,1,1024,128]{3,2,1,0:T(8,128)(2,1)S(1)}, u32[]{:S(2)}, u32[]{:S(2)}) collective-permute-start(bf16[1,1,1024,128]{3,2,1,0:T(8,128)(2,1)S(1)} %collective-permute-done), channel_id=1, source_target_pairs={{0,1},{1,2},{2,3},{3,4},{4,5},{5,6},{6,7},{7,0},{8,9},{9,10},{10,1... | collective-permute-start | bytes 786440 | tf_op jit(solution)/shard_map/ppermute | solution.py:16
  14.0 9.2 %collective-permute-start.2 = (bf16[1,1,1024,128]{3,2,1,0:T(8,128)(2,1)S(1)}, bf16[1,1,1024,128]{3,2,1,0:T(8,128)(2,1)S(1)}, u32[]{:S(2)}, u32[]{:S(2)}) collective-permute-start(bf16[1,1,1024,128]{3,2,1,0:T(8,128)(2,1)S(1)} %collective-permute-done.1), channel_id=1, source_target_pairs={{0,1},{1,2},{2,3},{3,4},{4,5},{5,6},{6,7},{7,0},{8,9},{9,10},{10,1... | collective-permute-start | bytes 786440 | tf_op jit(solution)/shard_map/ppermute | solution.py:16
  18.3 10.0 %collective-permute-start.5 = (bf16[1,1,1024,128]{3,2,1,0:T(8,128)(2,1)S(1)}, bf16[1,1,1024,128]{3,2,1,0:T(8,128)(2,1)S(1)}, u32[]{:S(2)}, u32[]{:S(2)}) collective-permute-start(bf16[1,1,1024,128]{3,2,1,0:T(8,128)(2,1)S(1)} %collective-permute-done.4), channel_id=1, source_target_pairs={{0,7},{1,0},{2,1},{3,2},{4,3},{5,4},{6,5},{7,6},{8,15},{9,8},{10,9... | collective-permute-start | bytes 786440 | tf_op jit(solution)/shard_map/ppermute | solution.py:18
  23.2 8.6 %collective-permute-start.3 = (bf16[1,1,1024,128]{3,2,1,0:T(8,128)(2,1)S(1)}, bf16[1,1,1024,128]{3,2,1,0:T(8,128)(2,1)S(1)}, u32[]{:S(2)}, u32[]{:S(2)}) collective-permute-start(bf16[1,1,1024,128]{3,2,1,0:T(8,128)(2,1)S(1)} %collective-permute-done.2), channel_id=1, source_target_pairs={{0,1},{1,2},{2,3},{3,4},{4,5},{5,6},{6,7},{7,0},{8,9},{9,10},{10,1... | collective-permute-start | bytes 786440 | tf_op jit(solution)/shard_map/ppermute | solution.py:16
  28.3 6.7 %collective-permute-start.6 = (bf16[1,1,1024,128]{3,2,1,0:T(8,128)(2,1)S(1)}, bf16[1,1,1024,128]{3,2,1,0:T(8,128)(2,1)S(1)}, u32[]{:S(2)}, u32[]{:S(2)}) collective-permute-start(bf16[1,1,1024,128]{3,2,1,0:T(8,128)(2,1)S(1)} %collective-permute-done.5), channel_id=1, source_target_pairs={{0,7},{1,0},{2,1},{3,2},{4,3},{5,4},{6,5},{7,6},{8,15},{9,8},{10,9... | collective-permute-start | bytes 786440 | tf_op jit(solution)/shard_map/ppermute | solution.py:18
  56.0 4.4 %collective-permute-start.7 = (bf16[1,32,2,64]{3,2,1,0:T(2,128)(2,1)S(1)}, bf16[1,32,2,64]{3,2,1,0:T(2,128)(2,1)S(1)}, u32[]{:S(2)}, u32[]{:S(2)}) collective-permute-start(bf16[1,32,2,64]{3,2,1,0:T(2,128)(2,1)S(1)} %slice.421), channel_id=1, source_target_pairs={{0,8},{8,16},{16,24},{24,0},{1,9},{9,17},{17,25},{25,1},{2,10},{10... | collective-permute-start | bytes 24584 | tf_op jit(solution)/shard_map/ppermute | solution.py:30
  56.8 4.1 %collective-permute-start.8 = (bf16[1,32,2,64]{3,2,1,0:T(2,128)(2,1)S(1)}, bf16[1,32,2,64]{3,2,1,0:T(2,128)(2,1)S(1)}, u32[]{:S(2)}, u32[]{:S(2)}) collective-permute-start(bf16[1,32,2,64]{3,2,1,0:T(2,128)(2,1)S(1)} %slice.423), channel_id=1, source_target_pairs={{8,0},{16,8},{24,16},{0,24},{9,1},{17,9},{25,17},{1,25},{10,2},{18... | collective-permute-start | bytes 24584 | tf_op jit(solution)/shard_map/ppermute | solution.py:31
  61.0 4.1 %collective-permute-start.10 = (bf16[34,1,2,64]{3,2,1,0:T(2,128)(2,1)S(1)}, bf16[34,1,2,64]{3,2,1,0:T(2,128)(2,1)S(1)}, u32[]{:S(2)}, u32[]{:S(2)}) collective-permute-start(bf16[34,1,2,64]{3,2,1,0:T(2,128)(2,1)S(1)} %get-tuple-element.50), channel_id=1, source_target_pairs={{1,0},{2,1},{3,2},{4,3},{5,4},{6,5},{7,6},{0,7},{9,8},{10,9},{11,1... | collective-permute-start | bytes 26120 | tf_op jit(solution)/shard_map/ppermute | solution.py:31
  61.0 4.1 %collective-permute-start.9 = (bf16[34,1,2,64]{3,2,1,0:T(2,128)(2,1)S(1)}, bf16[34,1,2,64]{3,2,1,0:T(2,128)(2,1)S(1)}, u32[]{:S(2)}, u32[]{:S(2)}) collective-permute-start(bf16[34,1,2,64]{3,2,1,0:T(2,128)(2,1)S(1)} %get-tuple-element.49), channel_id=1, source_target_pairs={{0,1},{1,2},{2,3},{3,4},{4,5},{5,6},{6,7},{7,0},{8,9},{9,10},{10,1... | collective-permute-start | bytes 26120 | tf_op jit(solution)/shard_map/ppermute | solution.py:30
  74.1 4.4 %collective-permute-start.11 = (bf16[1,32,2,128]{3,2,1,0:T(2,128)(2,1)S(1)}, bf16[1,32,2,128]{3,2,1,0:T(2,128)(2,1)S(1)}, u32[]{:S(2)}, u32[]{:S(2)}) collective-permute-start(bf16[1,32,2,128]{3,2,1,0:T(2,128)(2,1)S(1)} %bitcast.371), channel_id=1, source_target_pairs={{0,8},{8,16},{16,24},{24,0},{1,9},{9,17},{17,25},{25,1},{2,10},{10... | collective-permute-start | bytes 49160 | tf_op jit(solution)/shard_map/ppermute | solution.py:30
  74.2 4.4 %collective-permute-start.12 = (bf16[1,32,2,128]{3,2,1,0:T(2,128)(2,1)S(1)}, bf16[1,32,2,128]{3,2,1,0:T(2,128)(2,1)S(1)}, u32[]{:S(2)}, u32[]{:S(2)}) collective-permute-start(bf16[1,32,2,128]{3,2,1,0:T(2,128)(2,1)S(1)} %bitcast.369), channel_id=1, source_target_pairs={{8,0},{16,8},{24,16},{0,24},{9,1},{17,9},{25,17},{1,25},{10,2},{18... | collective-permute-start | bytes 49160 | tf_op jit(solution)/shard_map/ppermute | solution.py:31
  78.6 4.7 %collective-permute-start.13 = (bf16[34,1,2,128]{3,2,1,0:T(2,128)(2,1)S(1)}, bf16[34,1,2,128]{3,2,1,0:T(2,128)(2,1)S(1)}, u32[]{:S(2)}, u32[]{:S(2)}) collective-permute-start(bf16[34,1,2,128]{3,2,1,0:T(2,128)(2,1)S(1)} %get-tuple-element.47), channel_id=1, source_target_pairs={{0,1},{1,2},{2,3},{3,4},{4,5},{5,6},{6,7},{7,0},{8,9},{9,10},{10,1... | collective-permute-start | bytes 52232 | tf_op jit(solution)/shard_map/ppermute | solution.py:30
  82.5 4.1 %collective-permute-start.14 = (bf16[34,1,2,128]{3,2,1,0:T(2,128)(2,1)S(1)}, bf16[34,1,2,128]{3,2,1,0:T(2,128)(2,1)S(1)}, u32[]{:S(2)}, u32[]{:S(2)}) collective-permute-start(bf16[34,1,2,128]{3,2,1,0:T(2,128)(2,1)S(1)} %get-tuple-element.48), channel_id=1, source_target_pairs={{1,0},{2,1},{3,2},{4,3},{5,4},{6,5},{7,6},{0,7},{9,8},{10,9},{11,1... | collective-permute-start | bytes 52232 | tf_op jit(solution)/shard_map/ppermute | solution.py:31
  97.0 4.6 %collective-permute-start.15 = (bf16[1,16,2,128]{3,2,1,0:T(2,128)(2,1)S(1)}, bf16[1,16,2,128]{3,2,1,0:T(2,128)(2,1)S(1)}, u32[]{:S(2)}, u32[]{:S(2)}) collective-permute-start(bf16[1,16,2,128]{3,2,1,0:T(2,128)(2,1)S(1)} %get-tuple-element.81), channel_id=1, source_target_pairs={{0,8},{8,16},{16,24},{24,0},{1,9},{9,17},{17,25},{25,1},{2,10},{10... | collective-permute-start | bytes 24584 | tf_op jit(solution)/shard_map/ppermute | solution.py:30
  97.5 4.1 %collective-permute-start.16 = (bf16[1,16,2,128]{3,2,1,0:T(2,128)(2,1)S(1)}, bf16[1,16,2,128]{3,2,1,0:T(2,128)(2,1)S(1)}, u32[]{:S(2)}, u32[]{:S(2)}) collective-permute-start(bf16[1,16,2,128]{3,2,1,0:T(2,128)(2,1)S(1)} %get-tuple-element.82), channel_id=1, source_target_pairs={{8,0},{16,8},{24,16},{0,24},{9,1},{17,9},{25,17},{1,25},{10,2},{18... | collective-permute-start | bytes 24584 | tf_op jit(solution)/shard_map/ppermute | solution.py:31
  102.6 4.0 %collective-permute-start.18 = (bf16[18,1,2,128]{3,2,1,0:T(2,128)(2,1)S(1)}, bf16[18,1,2,128]{3,2,1,0:T(2,128)(2,1)S(1)}, u32[]{:S(2)}, u32[]{:S(2)}) collective-permute-start(bf16[18,1,2,128]{3,2,1,0:T(2,128)(2,1)S(1)} %get-tuple-element.78), channel_id=1, source_target_pairs={{1,0},{2,1},{3,2},{4,3},{5,4},{6,5},{7,6},{0,7},{9,8},{10,9},{11,1... | collective-permute-start | bytes 27656 | tf_op jit(solution)/shard_map/ppermute | solution.py:31
  109.3 4.7 %collective-permute-start.19 = (bf16[1,16,2,128]{3,2,1,0:T(2,128)(2,1)S(1)}, bf16[1,16,2,128]{3,2,1,0:T(2,128)(2,1)S(1)}, u32[]{:S(2)}, u32[]{:S(2)}) collective-permute-start(bf16[1,16,2,128]{3,2,1,0:T(2,128)(2,1)S(1)} %bitcast.374), channel_id=1, source_target_pairs={{0,8},{8,16},{16,24},{24,0},{1,9},{9,17},{17,25},{25,1},{2,10},{10... | collective-permute-start | bytes 24584 | tf_op jit(solution)/shard_map/ppermute | solution.py:30
  115.0 4.0 %collective-permute-start.22 = (bf16[18,1,2,128]{3,2,1,0:T(2,128)(2,1)S(1)}, bf16[18,1,2,128]{3,2,1,0:T(2,128)(2,1)S(1)}, u32[]{:S(2)}, u32[]{:S(2)}) collective-permute-start(bf16[18,1,2,128]{3,2,1,0:T(2,128)(2,1)S(1)} %get-tuple-element.76), channel_id=1, source_target_pairs={{1,0},{2,1},{3,2},{4,3},{5,4},{6,5},{7,6},{0,7},{9,8},{10,9},{11,1... | collective-permute-start | bytes 27656 | tf_op jit(solution)/shard_map/ppermute | solution.py:31
  122.2 5.0 %collective-permute-start.23 = (bf16[1,32,2,256]{3,2,1,0:T(2,128)(2,1)S(1)}, bf16[1,32,2,256]{3,2,1,0:T(2,128)(2,1)S(1)}, u32[]{:S(2)}, u32[]{:S(2)}) collective-permute-start(bf16[1,32,2,256]{3,2,1,0:T(2,128)(2,1)S(1)} %get-tuple-element.16), channel_id=1, source_target_pairs={{0,8},{8,16},{16,24},{24,0},{1,9},{9,17},{17,25},{25,1},{2,10},{10... | collective-permute-start | bytes 98312 | tf_op jit(solution)/shard_map/ppermute | solution.py:30
  128.2 4.3 %collective-permute-start.26 = (bf16[34,1,2,256]{3,2,1,0:T(2,128)(2,1)S(1)}, bf16[34,1,2,256]{3,2,1,0:T(2,128)(2,1)S(1)}, u32[]{:S(2)}, u32[]{:S(2)}) collective-permute-start(bf16[34,1,2,256]{3,2,1,0:T(2,128)(2,1)S(1)} %get-tuple-element.15), channel_id=1, source_target_pairs={{1,0},{2,1},{3,2},{4,3},{5,4},{6,5},{7,6},{0,7},{9,8},{10,9},{11,1... | collective-permute-start | bytes 104456 | tf_op jit(solution)/shard_map/ppermute | solution.py:31
  170.5 4.8 %collective-permute-start.27 = (bf16[1,32,2,128]{3,2,1,0:T(2,128)(2,1)S(1)}, bf16[1,32,2,128]{3,2,1,0:T(2,128)(2,1)S(1)}, u32[]{:S(2)}, u32[]{:S(2)}) collective-permute-start(bf16[1,32,2,128]{3,2,1,0:T(2,128)(2,1)S(1)} %bitcast.372), channel_id=1, source_target_pairs={{0,8},{8,16},{16,24},{24,0},{1,9},{9,17},{17,25},{25,1},{2,10},{10... | collective-permute-start | bytes 49160 | tf_op jit(solution)/shard_map/ppermute | solution.py:30
  176.4 4.1 %collective-permute-start.30 = (bf16[34,1,2,128]{3,2,1,0:T(2,128)(2,1)S(1)}, bf16[34,1,2,128]{3,2,1,0:T(2,128)(2,1)S(1)}, u32[]{:S(2)}, u32[]{:S(2)}) collective-permute-start(bf16[34,1,2,128]{3,2,1,0:T(2,128)(2,1)S(1)} %get-tuple-element.46), channel_id=1, source_target_pairs={{1,0},{2,1},{3,2},{4,3},{5,4},{6,5},{7,6},{0,7},{9,8},{10,9},{11,1... | collective-permute-start | bytes 52232 | tf_op jit(solution)/shard_map/ppermute | solution.py:31
  (19 other events, 295.9 us)
